TPU v7x, 256 devices: a whole 4x4x8 slice. The times are simulated.
256 devices in a mesh: grp: 16 (over z, core), dp: 8 (over y, x_hi), head: 2 (over x_lo).
Axes of the slice: x: 4 (x_hi: 2, x_lo: 2; x = x_hi * 2 + x_lo), y: 4, z: 8, core: 2. Of those that a mesh axis runs over, the one named last changes fastest.
Arguments:
- queries: bfloat16 [16384, 4096], P(('dp', 'grp'), 'head'), parts along dimension 0, may hold values from -5 to 5
- out_grad: bfloat16 [16384, 4096], P(('dp', 'grp'), 'head'), parts along dimension 0, may hold values from -24 to 24
- resp_keys: bfloat16 [16384, 1024], P(('dp', 'grp'), 'head'), parts along dimension 0, may hold values from -10 to 10
- response_values: bfloat16 [16384, 1024], P(('dp', 'grp'), 'head'), parts along dimension 0, may hold values from -12 to 12
- prompt_keys: bfloat16 [16384, 1024], P(('dp', 'grp'), 'head'), parts along dimension 0, may hold values from -10 to 10
- prompt_value_rows: bfloat16 [16384, 1024], P(('dp', 'grp'), 'head'), parts along dimension 0, may hold values from -12 to 12
- lengths: int32 [128], P(('dp', 'grp')), parts along dimension 0, may hold values from 1 to 128, 1536 in all
- tree_mask: int32 [128, 16], P(('dp', 'grp')), parts along dimension 0, may hold values from 0 to 1, as said below
- prompt_order: int32 [128], P('dp'), parts along dimension 0, may hold values from 0 to 15, as said below
Outputs:
- query_gradient: float32 [16384, 4096], P(('dp', 'grp'), 'head'), parts along dimension 0
- response_key_gradient: float32 [16384, 1024], P(('dp', 'grp'), 'head'), parts along dimension 0
- response_value_gradient: float32 [16384, 1024], P(('dp', 'grp'), 'head'), parts along dimension 0
- prompt_keygrad: float32 [16384, 1024], P(('dp', 'grp'), 'head'), parts along dimension 0
- prompt_valgrad: float32 [16384, 1024], P(('dp', 'grp'), 'head'), parts along dimension 0
There are 8 independent parts, one for each index of `dp`. A program takes and returns all parts, laid end to end along the dimension named above; each array names one. Nothing has to cross between parts.
Inputs may be any that keep to these rules, and one draw needn't show every extreme that they name: `tree_mask`: row g marks the tree tiles on the path from root tile 0 to one tile of a tree in which each tile's parent is an earlier tile; tile 0 is marked in every row and every tile is marked in some row. A permutation: prompt slot s (prompt tokens s * 128 to (s + 1) * 128 - 1) holds tree tile prompt_order[s]. `lengths`: some response has all 128 tokens live.
All inputs are finite; a program needn't handle non-finite values. No bound on the sum of `lengths` on one device may be relied on, other than what follows from the above.
Results may differ from a plain program's by a relative error of at most 0.0039.
Values may be sent and summed in bfloat16 or wider, within the bound.
A program may use at most 128 MiB of HBM per device.

v0:
```python
import math

import jax
import jax.numpy as jnp
from jax import lax
from jax.sharding import PartitionSpec as P

HEAD_WIDTH = 128
TILE = 128


masked_fill = -1e30


def block_total(row_total):
    pieces = 1
    while row_total % pieces != 0 or row_total // pieces > TILE:
        pieces = pieces + 1
    return pieces


def local(
    queries,
    out_grad,
    resp_keys,
    response_values,
    prompt_keys,
    prompt_value_rows,
    lengths,
    tree_mask,
    prompt_order,
):
    query_count = queries.shape[0]
    paired_width = resp_keys.shape[1]
    shared_heads = paired_width // HEAD_WIDTH
    group_members = queries.shape[1] // (HEAD_WIDTH * shared_heads)
    inv_root = 1.0 / math.sqrt(HEAD_WIDTH)
    query_halves = queries.reshape(query_count, shared_heads, group_members, HEAD_WIDTH)
    gradient_split = out_grad.reshape(query_count, shared_heads, group_members, HEAD_WIDTH)
    tile_total = tree_mask.shape[1]
    tile_ids = jnp.arange(tile_total)
    slot_seen = jnp.sum(
        jnp.where(prompt_order[:, None] == tile_ids[None, :], tree_mask[0][None, :], 0), axis=1
    )
    position = jnp.arange(query_count)
    live_rows = position < lengths[0]
    causal = position[None, :] <= position[:, None]

    def prompt_seen(first_row, row_span):
        slot_ids = (first_row + jnp.arange(row_span)) // TILE
        slot_hit = (
            jnp.sum(
                jnp.where(slot_ids[:, None] == tile_ids[None, :], slot_seen[None, :], 0), axis=1
            )
            > 0
        )
        return jnp.broadcast_to(slot_hit[None, :], (query_count, row_span))

    def guarded(compute):
        result = compute()
        return result

    def scores_of(rows_of_keys):
        head_keys = rows_of_keys.reshape(rows_of_keys.shape[0], shared_heads, HEAD_WIDTH)
        return (
            jnp.einsum(
                "rkgd,lkd->kgrl", query_halves, head_keys, preferred_element_type=jnp.float32
            )
            * inv_root
        )

    def grad_dot_of(rows_of_values):
        head_values = rows_of_values.reshape(rows_of_values.shape[0], shared_heads, HEAD_WIDTH)
        return jnp.einsum(
            "rkgd,lkd->kgrl", gradient_split, head_values, preferred_element_type=jnp.float32
        )

    def stats_step(running, rows_of_keys, rows_of_values, allowed):
        run_max, exp_total, weighted = running
        scores = scores_of(rows_of_keys)
        grad_dot = grad_dot_of(rows_of_values)
        new_max = jnp.maximum(run_max, jnp.max(jnp.where(allowed, scores, masked_fill), axis=-1))
        factor = jnp.exp(run_max - new_max)
        shifted = jnp.exp(jnp.where(allowed, scores - new_max[..., None], masked_fill))
        return (
            new_max,
            factor * exp_total + jnp.sum(shifted, axis=-1),
            factor * weighted + jnp.sum(shifted * grad_dot, axis=-1),
        )

    stat_shape = (shared_heads, group_members, query_count)
    initial = (
        jnp.full(stat_shape, masked_fill, jnp.float32),
        jnp.zeros(stat_shape, jnp.float32),
        jnp.zeros(stat_shape, jnp.float32),
    )
    running = stats_step(initial, resp_keys, response_values, causal)
    prompt_pair = (
        lax.all_gather(prompt_keys, "grp", axis=0, tiled=True),
        lax.all_gather(prompt_value_rows, "grp", axis=0, tiled=True),
    )
    rows_of_keys, rows_of_values = prompt_pair
    row_span = rows_of_keys.shape[0]
    pieces = block_total(row_span)
    prompt_block_rows = row_span // pieces

    def one_block(block_id, partial_value):
        offset = block_id * prompt_block_rows
        key_block = lax.dynamic_slice_in_dim(rows_of_keys, offset, prompt_block_rows, 0)
        value_block = lax.dynamic_slice_in_dim(rows_of_values, offset, prompt_block_rows, 0)
        allowed = prompt_seen(0 + offset, prompt_block_rows)
        return guarded(lambda: stats_step(partial_value, key_block, value_block, allowed))

    running = lax.fori_loop(0, pieces, one_block, running)
    run_max, exp_total, weighted = running
    log_total = run_max + jnp.log(exp_total)
    row_delta = weighted / exp_total

    def pair_terms(rows_of_keys, rows_of_values, allowed):
        scores = scores_of(rows_of_keys)
        grad_dot = grad_dot_of(rows_of_values)
        live = allowed & live_rows[:, None]
        attn_prob = jnp.exp(jnp.where(live, scores - log_total[..., None], masked_fill))
        dscore = (attn_prob * (grad_dot - row_delta[..., None])).astype(jnp.bfloat16)
        return (attn_prob.astype(jnp.bfloat16), dscore)

    def query_term(dscore, rows_of_keys):
        head_keys = rows_of_keys.reshape(rows_of_keys.shape[0], shared_heads, HEAD_WIDTH)
        return (
            jnp.einsum("kgrl,lkd->rkgd", dscore, head_keys, preferred_element_type=jnp.float32)
            * inv_root
        )

    def key_value_terms(prob_half, dscore):
        key_part = (
            jnp.einsum("kgrl,rkgd->lkd", dscore, query_halves, preferred_element_type=jnp.float32)
            * inv_root
        )
        value_part = jnp.einsum(
            "kgrl,rkgd->lkd", prob_half, gradient_split, preferred_element_type=jnp.float32
        )
        key_count = key_part.shape[0]
        return (
            key_part.reshape(key_count, paired_width),
            value_part.reshape(key_count, paired_width),
        )

    prob_half, dscore = pair_terms(resp_keys, response_values, causal)
    query_local = query_term(dscore, resp_keys)
    response_key_gradient, response_value_gradient = key_value_terms(prob_half, dscore)
    prompt_keyrows, prompt_valrows = prompt_pair
    prompt_rows = prompt_keyrows.shape[0]
    pieces = block_total(prompt_rows)
    block_rows = prompt_rows // pieces
    zero_query = jnp.zeros(query_halves.shape, jnp.float32)

    def grad_block(block_id, partial_value):
        offset = block_id * block_rows
        key_block = lax.dynamic_slice_in_dim(prompt_keyrows, offset, block_rows, 0)
        value_block = lax.dynamic_slice_in_dim(prompt_valrows, offset, block_rows, 0)
        allowed = prompt_seen(offset, block_rows)

        def compute():
            block_prob, block_score = pair_terms(key_block, value_block, allowed)
            key_part, value_part = key_value_terms(block_prob, block_score)
            return (
                partial_value[0] + query_term(block_score, key_block),
                lax.dynamic_update_slice_in_dim(partial_value[1], key_part, offset, 0),
                lax.dynamic_update_slice_in_dim(partial_value[2], value_part, offset, 0),
            )

        return guarded(compute)

    zero_rows = jnp.zeros((prompt_rows, paired_width), jnp.float32)
    query_prompt, key_partial, value_partial = lax.fori_loop(
        0, pieces, grad_block, (zero_query, zero_rows, zero_rows)
    )
    prompt_keygrad, prompt_valgrad = (
        lax.psum_scatter(key_partial, "grp", scatter_dimension=0, tiled=True),
        lax.psum_scatter(value_partial, "grp", scatter_dimension=0, tiled=True),
    )
    query_gradient = (query_local + query_prompt).reshape(query_count, queries.shape[1])
    return (
        query_gradient,
        response_key_gradient,
        response_value_gradient,
        prompt_keygrad,
        prompt_valgrad,
    )


def solution(mesh):
    return jax.shard_map(
        local,
        mesh=mesh,
        in_specs=(
            P(("dp", "grp"), "head"),
            P(("dp", "grp"), "head"),
            P(("dp", "grp"), "head"),
            P(("dp", "grp"), "head"),
            P(("dp", "grp"), "head"),
            P(("dp", "grp"), "head"),
            P(("dp", "grp")),
            P(("dp", "grp"), None),
            P("dp"),
        ),
        out_specs=(
            P(("dp", "grp"), "head"),
            P(("dp", "grp"), "head"),
            P(("dp", "grp"), "head"),
            P(("dp", "grp"), "head"),
            P(("dp", "grp"), "head"),
        ),
        check_vma=False,
    )
```

profile of v0, /device:TPU:1, one launch (start us, length us, event | category | flops | bytes accessed | tf_op | source)
XLA Modules:
  0.0 378.5 jit_solution(11139195773777964908)
XLA Ops:
  7.2 1.7 copy.80
  9.0 1.7 copy.81
  12.8 1.3 copy.74
  14.4 1.3 copy.77
  17.2 1.0 copy-done
  18.2 1.3 multiply_reduce_fusion
  19.5 36.0 %all-gather.3.cloned.1.call-done = bf16[2048,512]{0,1:T(8,128)(2,1)} async-done(((bf16[128,512]{0,1:T(8,128)(2,1)}), bf16[2048,512]{0,1:T(8,128)(2,1)}) %all-gather.3.cloned.1.call-update) | async-done | bytes 2097168 | tf_op jit(solution)/shard_map/all_gather | solution.py:99
  55.5 42.5 %all-gather.5.cloned.1.call-done = bf16[2048,512]{0,1:T(8,128)(2,1)} async-done(((bf16[128,512]{0,1:T(8,128)(2,1)}), bf16[2048,512]{0,1:T(8,128)(2,1)}) %all-gather.5.cloned.1.call-update) | async-done | bytes 2097168 | tf_op jit(solution)/shard_map/all_gather | solution.py:100
  98.0 46.1 %while.40 = (s32[]{:T(128)}, f32[4,4,128]{2,1,0:T(4,128)S(1)}, f32[4,4,128]{2,1,0:T(4,128)S(1)}, f32[4,4,128]{2,1,0:T(4,128)S(1)}, s32[16]{0:T(128)}, /*index=5*...) while((s32[]{:T(128)}, f32[4,4,128]{2,1,0:T(4,128)S(1)}, ...), condition=%wide.region_9.10_spmd.clone, body=%wide.region_4.9_spmd.clone.sunk | while | flops 136853504 | bytes 5130995 | solution.py:114
  98.7 1.0 constant_dynamic-slice_fusion.7
  104.5 1.0 constant_dynamic-slice_fusion.7
  107.4 1.0 constant_dynamic-slice_fusion.7
  113.1 1.0 constant_dynamic-slice_fusion.7
  118.9 1.0 constant_dynamic-slice_fusion.7
  121.8 1.0 constant_dynamic-slice_fusion.7
  127.5 1.0 constant_dynamic-slice_fusion.7
  136.2 1.0 constant_dynamic-slice_fusion.7
  144.1 2.5 broadcast_in_dim.220.clone2
  146.6 2.5 broadcast_in_dim.220.clone
  149.1 100.0 %while.41 = (s32[]{:T(128)}, f32[128,4,4,128]{0,3,2,1:T(8,128)S(1)}, f32[2048,512]{1,0:T(8,128)}, f32[2048,512]{1,0:T(8,128)}, bf16[2048,512]{0,1:T(8,128)(2,1)}...) while((s32[]{:T(128)}, ...), condition=%wide.region_12.13_spmd.clone, body=%wide.region_10.12_spmd.clone.sunk | while | flops 338256000 | bytes 12503849 | solution.py:175
  251.8 1.5 multiply_convert_fusion
  254.8 1.3 copy.90
  256.1 51.7 %reduce-scatter.5.cloned.1.call-done = f32[128,512]{1,0:T(8,128)} async-done(((f32[2048,512]{1,0:T(8,128)}), f32[128,512]{1,0:T(8,128)}) %reduce-scatter.5.cloned.1.call-update) | async-done | bytes 262160 | tf_op jit(solution)/shard_map/reduce_scatter | solution.py:180
  307.8 64.2 %reduce-scatter.3.cloned.1.call-done = f32[128,512]{1,0:T(8,128)} async-done(((f32[2048,512]{1,0:T(8,128)}), f32[128,512]{1,0:T(8,128)}) %reduce-scatter.3.cloned.1.call-update) | async-done | bytes 262160 | tf_op jit(solution)/shard_map/reduce_scatter | solution.py:179
  (432 shorter events, 143.4 us)
Async XLA Ops:
  7.2 8.9 %copy-start.6 = (s32[16]{0:T(128)S(1)}, s32[16]{0:T(128)}, u32[]{:S(2)}) copy-start(s32[16]{0:T(128)} %param.21) | copy-start | bytes 196
  7.2 8.9 %copy-start.5 = (s32[1,16]{1,0:T(1,128)S(1)}, s32[1,16]{1,0:T(1,128)}, u32[]{:S(2)}) copy-start(s32[1,16]{1,0:T(1,128)} %param.20) | copy-start | bytes 196
  7.2 48.3 %all-gather.3.cloned.1.call-start = ((), (), s32[]{:S(2)}) async-start(), calls=%async_computation.2 | async-start | bytes 2228224 | tf_op jit(solution)/shard_map/all_gather | solution.py:99
  8.9 89.1 %all-gather.5.cloned.1.call-start = ((), (), s32[]{:S(2)}) async-start(), calls=%async_computation.3 | async-start | bytes 2228224 | tf_op jit(solution)/shard_map/all_gather | solution.py:100
  10.7 297.1 %reduce-scatter.5.cloned.1.call-start = ((), (), s32[]{:S(2)}) async-start(), calls=%async_computation.5 | async-start | bytes 4456448 | tf_op jit(solution)/shard_map/reduce_scatter | solution.py:180
  11.8 5.4 %copy-start.2 = (bf16[128,4,128,1]{0,2,3,1:T(8,128)(2,1)}, bf16[128,4,128,1]{0,2,3,1:T(8,128)(2,1)S(1)}, u32[]{:S(2)}) copy-start(bf16[128,4,128,1]{0,2,3,1:T(8,128)(2,1)S(1)} %copy.110) | copy-start | bytes 393220
  17.2 1.1 copy-start
  249.1 1.3 copy-start.1
  249.1 122.9 %reduce-scatter.3.cloned.1.call-start = ((), (), s32[]{:S(2)}) async-start(), calls=%async_computation.4 | async-start | bytes 4456448 | tf_op jit(solution)/shard_map/reduce_scatter | solution.py:179
  249.7 4.8 %copy-start.3 = (bf16[128,4,128,1]{0,2,3,1:T(8,128)(2,1)S(1)}, bf16[128,4,128,1]{0,2,3,1:T(8,128)(2,1)}, u32[]{:S(2)}) copy-start(bf16[128,4,128,1]{0,2,3,1:T(8,128)(2,1)} %copy-done.2) | copy-start | bytes 393220
  250.4 0.6 copy-start.4
Sparse Core Ops, SparseCore 0:
  10.3 45.1 all-gather.2
  57.9 40.0 all-gather.4
  249.2 58.5 reduce-scatter.4
  310.7 61.2 reduce-scatter.2
where the time goes:
time: 382 us; the launch traced here: 379 us
  waiting for transfers between devices  195 us (51%)
  local copies, waits for them, and re-layouts  80.6 us (21%)
  matrix products  44.3 us (12%)
  other arithmetic  41.7 us (11%)
  between operations  14.6 us (4%)
    reduce_scatter x1, waiting for transfers between devices, local(): lax.psum_scatter(key_partial, 'grp', scatter_dimension=0, tiled=True)  64.2 us
    reduce_scatter x1, waiting for transfers between devices, local(): lax.psum_scatter(value_partial, 'grp', scatter_dimension=0, tiled=True)  51.7 us
    all_gather x1, waiting for transfers between devices, local(): lax.all_gather(prompt_value_rows, 'grp', axis=0, tiled=True)  42.5 us
    all_gather x1, waiting for transfers between devices, local(): lax.all_gather(prompt_keys, 'grp', axis=0, tiled=True)  36 us
    reduce_sum x32, other arithmetic, prompt_seen(): jnp.sum(jnp.where(slot_ids[:, None] == tile_ids[None, :], slot_seen[None,...  22.6 us
    dynamic_slice x16, local copies, waits for them, and re-layouts, one_block(): lax.dynamic_slice_in_dim(rows_of_keys, offset, prompt_block_rows, 0)  15.8 us
    dynamic_update_slice x32, local copies, waits for them, and re-layouts, compute(): lax.dynamic_update_slice_in_dim(partial_value[2], value_part, offset, 0)  15.3 us
    dynamic_slice x16, local copies, waits for them, and re-layouts, grad_block(): key_block = lax.dynamic_slice_in_dim(prompt_keyrows, offset, block_rows, 0)  14.7 us
  transfers between devices with their start and end apart: 4, of which 4 were waited for; matrix products, arithmetic and copies ran while one was open for 4% of the time, Pallas kernels for 0%

commit v1 on v0

v1 whole, which is shorter than its diff:
```python
import functools
import math

import jax
import jax.numpy as jnp
from jax import lax
from jax.experimental import pallas as pl
from jax.experimental.pallas import tpu as pltpu
from jax.sharding import PartitionSpec as P

MESH = pl.DeviceIdType.MESH
WIDTH = 128
RING = 8
HEADS = 2
MEMBERS = 4
HALF = MEMBERS * WIDTH
ROWS = 2 * HALF
CHUNK = 2 * WIDTH
LANES = 256
UP, DOWN = 0, 1
KEY, VALUE = 0, 1
HOPS = ((4, 3), (3, 4))
ROOT = 1.0 / math.sqrt(WIDTH)
SCALE = ROOT * math.log2(math.e)
HIDDEN = -1e30


def dot_nt(a, b):
    return lax.dot_general(a, b, (((1,), (1,)), ((), ())), preferred_element_type=jnp.float32)


def dot_nn(a, b):
    return jnp.dot(a, b, preferred_element_type=jnp.float32)


def dot_tn(a, b):
    return lax.dot_general(a, b, (((0,), (0,)), ((), ())), preferred_element_type=jnp.float32)


def slot_of(direction, hop):
    return hop if direction == UP else RING - hop


def kernel(
    q_ref, og_ref, rk_ref, rv_ref, pk_ref, pv_ref, len_ref, mask_ref, order_ref,
    dq_out, drk_out, drv_out, dpk_out, dpv_out,
    qin, oin, rkin, rvin, meta, qs, os_, kv,
    e_buf, d_buf, er_buf, dr_buf, m_run, l_run, w_run, m_save, mr_save, p_tmp, ds_buf, dsr_buf,
    grad, sbuf, rbuf, fin, mate_grad, dq_t, dq_stage, drk_stage, drv_stage,
    loc_sem, pair_send, pair_recv, ag_send, ag_recv, rs_send, rs_recv,
):
    me = lax.axis_index("grp")
    z, c = me // 2, me % 2
    other = 1 - c
    above, below = (z + 1) % RING, (z + RING - 1) % RING
    straight = (above * 2 + c, below * 2 + c)
    cross = (above * 2 + other, below * 2 + other)
    mate = z * 2 + other

    def remote(src, dst, send, recv, target):
        return pltpu.make_async_remote_copy(
            src_ref=src, dst_ref=dst, send_sem=send, recv_sem=recv,
            device_id={"grp": target}, device_id_type=MESH,
        )

    def cols(core, width, start=0, size=None):
        size = width if size is None else size
        return pl.ds(pl.multiple_of(core * width + start, WIDTH), size)

    def half(core):
        return pl.ds(pl.multiple_of(core * WIDTH, WIDTH), WIDTH)

    prompt = (pk_ref, pv_ref)

    local = [
        pltpu.make_async_copy(q_ref.at[:, cols(c, 1024)], qin.at[0], loc_sem.at[0]),
        pltpu.make_async_copy(og_ref.at[:, cols(c, 1024)], oin.at[0], loc_sem.at[1]),
        pltpu.make_async_copy(rk_ref.at[:, cols(c, 256)], rkin.at[0], loc_sem.at[2]),
        pltpu.make_async_copy(rv_ref.at[:, cols(c, 256)], rvin.at[0], loc_sem.at[3]),
    ]
    for t in range(2):
        for hh in range(HEADS):
            local.append(
                pltpu.make_async_copy(
                    prompt[t].at[:, cols(c, 256, hh * WIDTH, WIDTH)],
                    kv.at[t, hh, 0, half(c)],
                    loc_sem.at[4 + t * HEADS + hh],
                )
            )
    for copy in local:
        copy.start()

    for s in range(16):
        seen = mask_ref[0, order_ref[s]]
        row = jnp.full((1, LANES), seen, jnp.int32).astype(jnp.float32)
        meta[0, pl.ds(s, 1), :] = (1.0 - jnp.minimum(row, 1.0)) * HIDDEN
    meta[0, pl.ds(16, 8), :] = jnp.full((8, LANES), len_ref[0], jnp.int32).astype(jnp.float32)

    barrier = pltpu.get_barrier_semaphore()
    for target in (*straight, *cross, mate):
        pl.semaphore_signal(barrier, inc=1, device_id={"grp": target}, device_id_type=MESH)
    pl.semaphore_wait(barrier, 5)

    sends = []

    def start(copy):
        copy.start()
        sends.append(copy)
        return copy

    def first_hop(hh):
        for t in range(2):
            for d in (UP, DOWN):
                slot = slot_of(d, 1)
                for way, (core, target) in enumerate(((c, straight[d]), (other, cross[d]))):
                    start(
                        remote(
                            prompt[t].at[:, cols(core, 256, hh * WIDTH, WIDTH)],
                            kv.at[t, hh, slot, half(c)],
                            ag_send.at[t, hh, d, way],
                            ag_recv.at[t, hh, d, way],
                            target,
                        )
                    )

    def pair(i, src, dst):
        return start(remote(src, dst, pair_send.at[i], pair_recv.at[i], mate))

    first_hop(0)
    pair_copies = [
        pair(0, rk_ref.at[:, cols(other, 256)], rkin.at[1]),
        pair(1, rv_ref.at[:, cols(other, 256)], rvin.at[1]),
        pair(2, meta.at[0], meta.at[1]),
        pair(3, q_ref.at[:, cols(other, 1024)], qin.at[1]),
        pair(4, og_ref.at[:, cols(other, 1024)], oin.at[1]),
    ]
    for t in range(2):
        for hh in range(HEADS):
            pair_copies.append(
                pair(
                    5 + t * HEADS + hh,
                    prompt[t].at[:, cols(other, 256, hh * WIDTH, WIDTH)],
                    kv.at[t, hh, 0, half(c)],
                )
            )
    first_hop(1)

    for copy in local:
        copy.wait()
    for i, copy in enumerate(pair_copies[:5]):
        copy.wait_recv()

    for hh in range(HEADS):
        for p in range(2):
            for g in range(MEMBERS):
                rows = pl.ds(p * HALF + g * WIDTH, WIDTH)
                lanes = pl.ds((hh * MEMBERS + g) * WIDTH, WIDTH)
                qs[hh, rows, :] = qin[p, :, lanes]
                os_[hh, rows, :] = oin[p, :, lanes]

    def own_block(hh):
        for p in range(2):
            keys = rkin[p, :, pl.ds(hh * WIDTH, WIDTH)]
            values = rvin[p, :, pl.ds(hh * WIDTH, WIDTH)]

            @pl.loop(0, HALF // LANES)
            def _(b):
                lanes = pl.ds(pl.multiple_of(b * LANES, LANES), LANES)
                rows = pl.ds(pl.multiple_of(p * HALF + b * LANES, LANES), LANES)
                s = dot_nt(keys, qs[hh, rows, :])
                dp = dot_nt(values, os_[hh, rows, :])
                key_at = lax.broadcasted_iota(jnp.int32, (WIDTH, LANES), 0)
                row_at = lax.broadcasted_iota(jnp.int32, (WIDTH, LANES), 1) % WIDTH
                s = jnp.where(key_at <= row_at, s * SCALE, HIDDEN)
                top = jnp.max(s, axis=0, keepdims=True)
                e = jnp.exp2(s - top)
                er_buf[hh, p, :, lanes] = e
                dr_buf[hh, p, :, lanes] = dp
                m_run[hh, :, rows] = top
                mr_save[hh, :, rows] = top
                l_run[hh, :, rows] = jnp.sum(e, axis=0, keepdims=True)
                w_run[hh, :, rows] = jnp.sum(e * dp, axis=0, keepdims=True)

    def tile_bias(p, slot, part):
        tile = ((z + RING - slot) % RING) * 2 + part
        return meta[p, pl.ds(tile, 1), :]

    def forward(hh, slot):
        for p in range(2):
            bias = [tile_bias(p, slot, part) for part in range(2)]

            @pl.loop(0, HALF // LANES)
            def _(b):
                lanes = pl.ds(pl.multiple_of(p * HALF + b * LANES, LANES), LANES)
                s = dot_nt(kv[KEY, hh, slot], qs[hh, lanes, :])
                dp = dot_nt(kv[VALUE, hh, slot], os_[hh, lanes, :])
                d_buf[hh, slot, :, lanes] = dp
                old = m_run[hh, :, lanes]
                top = old
                for part in range(2):
                    high = jnp.max(s[part * WIDTH : (part + 1) * WIDTH], axis=0, keepdims=True)
                    top = jnp.maximum(top, high * SCALE + bias[part])
                less = jnp.exp2(old - top)
                total = l_run[hh, :, lanes] * less
                weighted = w_run[hh, :, lanes] * less
                for part in range(2):
                    rows = slice(part * WIDTH, (part + 1) * WIDTH)
                    e = jnp.exp2(s[rows] * SCALE - (top - bias[part]))
                    e_buf[hh, slot, rows, lanes] = e
                    total = total + jnp.sum(e, axis=0, keepdims=True)
                    weighted = weighted + jnp.sum(e * dp[rows], axis=0, keepdims=True)
                m_run[hh, :, lanes] = top
                m_save[hh, slot, :, lanes] = top
                l_run[hh, :, lanes] = total
                w_run[hh, :, lanes] = weighted

    own_block(0)
    own_block(1)
    for copy in pair_copies[5:]:
        copy.wait_recv()
    forward(0, 0)
    forward(1, 0)

    for hop in range(1, 5):
        for hh in range(HEADS):
            for t in range(2):
                for d in (UP, DOWN):
                    if hop > HOPS[t][d]:
                        continue
                    slot = slot_of(d, hop)
                    here = kv.at[t, hh, slot]
                    if hop == 1:
                        for way, core in enumerate((c, other)):
                            part = kv.at[t, hh, slot, half(core)]
                            remote(
                                part, part, ag_send.at[t, hh, d, way], ag_recv.at[t, hh, d, way], straight[d]
                            ).wait_recv()
                    else:
                        remote(
                            here, here, ag_send.at[t, hh, d, hop], ag_recv.at[t, hh, d, hop], straight[d]
                        ).wait_recv()
                    if hop < HOPS[t][d]:
                        start(
                            remote(
                                here,
                                kv.at[t, hh, slot_of(d, hop + 1)],
                                ag_send.at[t, hh, d, hop + 1],
                                ag_recv.at[t, hh, d, hop + 1],
                                straight[d],
                            )
                        )
            forward(hh, hop)
            if hop < 4:
                forward(hh, RING - hop)

    for hh in range(HEADS):
        for p in range(2):
            for b in range(HALF // LANES):
                lanes = pl.ds(p * HALF + b * LANES, LANES)
                total = l_run[hh, :, lanes]
                w_run[hh, :, lanes] = w_run[hh, :, lanes] / total
                at = (lax.broadcasted_iota(jnp.int32, (1, LANES), 1) % WIDTH).astype(jnp.float32)
                live = at < meta[p, pl.ds(16, 1), :]
                l_run[hh, :, lanes] = jnp.where(live, 1.0 / total, 0.0)

    def backward(hh, slot, keep):
        @pl.loop(0, ROWS // LANES)
        def _(b):
            lanes = pl.ds(pl.multiple_of(b * LANES, LANES), LANES)
            factor = jnp.exp2(m_save[hh, slot, :, lanes] - m_run[hh, :, lanes]) * l_run[hh, :, lanes]
            prob = e_buf[hh, slot, :, lanes] * factor
            p_tmp[:, lanes] = prob.astype(jnp.bfloat16)
            ds = prob * (d_buf[hh, slot, :, lanes] - w_run[hh, :, lanes])
            ds_buf[hh, slot, :, lanes] = ds.astype(jnp.bfloat16)

        grad[KEY, hh, keep] = dot_nn(ds_buf[hh, slot], qs[hh])
        grad[VALUE, hh, keep] = dot_nn(p_tmp[...], os_[hh])

    def pass_on(t, hh, d, hop, keep):
        i = hop - 1
        if hop == 1:
            sbuf[t, hh, d, i] = grad[t, hh, keep].astype(jnp.bfloat16)
        else:
            arrived = rbuf.at[t, hh, d, i - 1]
            remote(
                arrived, arrived, rs_send.at[t, hh, d, i - 1], rs_recv.at[t, hh, d, i - 1], straight[d]
            ).wait_recv()
            sbuf[t, hh, d, i] = (grad[t, hh, keep] + arrived[...].astype(jnp.float32)).astype(jnp.bfloat16)
        if hop < HOPS[t][d]:
            start(
                remote(
                    sbuf.at[t, hh, d, i],
                    rbuf.at[t, hh, d, i],
                    rs_send.at[t, hh, d, i],
                    rs_recv.at[t, hh, d, i],
                    straight[d],
                )
            )
        else:
            for way, (core, target) in enumerate(((c, straight[d]), (other, cross[d]))):
                start(
                    remote(
                        sbuf.at[t, hh, d, i, half(core)],
                        fin.at[t, hh, d, way],
                        rs_send.at[t, hh, d, 3 + way],
                        rs_recv.at[t, hh, d, 3 + way],
                        target,
                    )
                )

    for hh in range(HEADS):
        backward(hh, 4, 0)
        pass_on(KEY, hh, UP, 1, 0)
        pass_on(VALUE, hh, DOWN, 1, 0)
    for away in (3, 2, 1):
        for hh in range(HEADS):
            backward(hh, RING - away, 0)
            backward(hh, away, 1)
            for t in ((VALUE, KEY) if away == 3 else (KEY, VALUE)):
                pass_on(t, hh, UP, HOPS[t][UP] - away + 1, 0)
            for t in (KEY, VALUE):
                pass_on(t, hh, DOWN, HOPS[t][DOWN] - away + 1, 1)

    mates = []
    for hh in range(HEADS):
        backward(hh, 0, 0)
        for t in range(2):
            mates.append(pair(9 + t * HEADS + hh, grad.at[t, hh, 0, half(other)], mate_grad.at[t, hh]))

    for hh in range(HEADS):
        lanes = pl.ds(hh * WIDTH, WIDTH)
        for p in range(2):
            rows = pl.ds(p * HALF, HALF)
            factor = jnp.exp2(mr_save[hh, :, rows] - m_run[hh, :, rows]) * l_run[hh, :, rows]
            prob = er_buf[hh, p] * factor
            ds = (prob * (dr_buf[hh, p] - w_run[hh, :, rows])).astype(jnp.bfloat16)
            dsr_buf[hh, p] = ds
            drk_stage[p, :, lanes] = dot_nn(ds, qs[hh, rows, :]) * ROOT
            drv_stage[p, :, lanes] = dot_nn(prob.astype(jnp.bfloat16), os_[hh, rows, :])
    outs = [
        pltpu.make_async_copy(drk_stage.at[0], drk_out.at[:, cols(c, 256)], loc_sem.at[0]),
        pltpu.make_async_copy(drv_stage.at[0], drv_out.at[:, cols(c, 256)], loc_sem.at[1]),
    ]
    for copy in outs:
        copy.start()
    mates.append(pair(13, drk_stage.at[1], drk_out.at[:, cols(c, 256)]))
    mates.append(pair(14, drv_stage.at[1], drv_out.at[:, cols(c, 256)]))

    for hh in range(HEADS):
        for p in range(2):
            for b in range(HALF // LANES):
                lanes = pl.ds(p * HALF + b * LANES, LANES)
                dq_t[...] = dot_tn(
                    rkin[p, :, pl.ds(hh * WIDTH, WIDTH)], dsr_buf[hh, p, :, pl.ds(b * LANES, LANES)]
                )

                @pl.loop(0, RING)
                def _(slot):
                    dq_t[...] += dot_tn(kv[KEY, hh, slot], ds_buf[hh, slot, :, lanes])

                for i in range(LANES // WIDTH):
                    g = hh * MEMBERS + b * (LANES // WIDTH) + i
                    block = dq_t[:, pl.ds(i * WIDTH, WIDTH)]
                    dq_stage[p, :, pl.ds(g * WIDTH, WIDTH)] = block.T * ROOT
    copy = pltpu.make_async_copy(dq_stage.at[0], dq_out.at[:, cols(c, 1024)], loc_sem.at[2])
    copy.start()
    outs.append(copy)
    mates.append(pair(15, dq_stage.at[1], dq_out.at[:, cols(c, 1024)]))

    for copy in mates[:4]:
        copy.wait_recv()
    result = (dpk_out, dpv_out)
    for hh in range(HEADS):
        for t in range(2):
            for way, core in enumerate((c, other)):
                share = grad[t, hh, 0, half(c), :] if way == 0 else mate_grad[t, hh]
                for d in (UP, DOWN):
                    arrived = fin.at[t, hh, d, way]
                    remote(
                        arrived, arrived, rs_send.at[t, hh, d, 3 + way], rs_recv.at[t, hh, d, 3 + way], straight[d]
                    ).wait_recv()
                    share = share + arrived[...].astype(jnp.float32)
                if t == KEY:
                    share = share * ROOT
                result[t][:, cols(core, 256, hh * WIDTH, WIDTH)] = share

    for copy in mates[4:]:
        copy.wait_recv()
    for copy in outs:
        copy.wait()
    for copy in sends:
        copy.wait_send()


def local(*args):
    bf16, f32 = jnp.bfloat16, jnp.float32
    vmem = pltpu.VMEM
    dma = pltpu.SemaphoreType.DMA
    any_ = pl.BlockSpec(memory_space=pl.ANY)
    smem = pl.BlockSpec(memory_space=pltpu.SMEM)
    in_vmem = pl.BlockSpec(memory_space=pltpu.VMEM)
    return pl.pallas_call(
        kernel,
        out_shape=(
            jax.ShapeDtypeStruct((WIDTH, 2048), f32),
            *(jax.ShapeDtypeStruct((WIDTH, 512), f32) for _ in range(4)),
        ),
        in_specs=[any_] * 6 + [smem] * 3,
        out_specs=(any_, any_, any_, in_vmem, in_vmem),
        scratch_shapes=[
            vmem((2, WIDTH, 1024), bf16),
            vmem((2, WIDTH, 1024), bf16),
            vmem((2, WIDTH, 256), bf16),
            vmem((2, WIDTH, 256), bf16),
            vmem((2, 24, LANES), f32),
            vmem((HEADS, ROWS, WIDTH), bf16),
            vmem((HEADS, ROWS, WIDTH), bf16),
            vmem((2, HEADS, RING, CHUNK, WIDTH), bf16),
            vmem((HEADS, RING, CHUNK, ROWS), f32),
            vmem((HEADS, RING, CHUNK, ROWS), f32),
            vmem((HEADS, 2, WIDTH, HALF), f32),
            vmem((HEADS, 2, WIDTH, HALF), f32),
            vmem((HEADS, 1, ROWS), f32),
            vmem((HEADS, 1, ROWS), f32),
            vmem((HEADS, 1, ROWS), f32),
            vmem((HEADS, RING, 1, ROWS), f32),
            vmem((HEADS, 1, ROWS), f32),
            vmem((CHUNK, ROWS), bf16),
            vmem((HEADS, RING, CHUNK, ROWS), bf16),
            vmem((HEADS, 2, WIDTH, HALF), bf16),
            vmem((2, HEADS, 2, CHUNK, WIDTH), f32),
            vmem((2, HEADS, 2, 4, CHUNK, WIDTH), bf16),
            vmem((2, HEADS, 2, 3, CHUNK, WIDTH), bf16),
            vmem((2, HEADS, 2, 2, WIDTH, WIDTH), bf16),
            vmem((2, HEADS, WIDTH, WIDTH), f32),
            vmem((WIDTH, LANES), f32),
            vmem((2, WIDTH, 1024), f32),
            vmem((2, WIDTH, 256), f32),
            vmem((2, WIDTH, 256), f32),
            dma((8,)),
            dma((16,)),
            dma((16,)),
            dma((2, HEADS, 2, 5)),
            dma((2, HEADS, 2, 5)),
            dma((2, HEADS, 2, 5)),
            dma((2, HEADS, 2, 5)),
        ],
        compiler_params=pltpu.CompilerParams(
            collective_id=0, has_side_effects=True, vmem_limit_bytes=60 * 1024 * 1024
        ),
        name="tree_attention_backward",
    )(*args)


def solution(mesh):
    rows = P(("dp", "grp"), "head")
    return jax.shard_map(
        local,
        mesh=mesh,
        in_specs=(rows,) * 6 + (P(("dp", "grp")), P(("dp", "grp"), None), P("dp")),
        out_specs=(rows,) * 5,
        check_vma=False,
    )
```

time: 382 us -> 80.3 us (0.21)
  waiting for transfers between devices: 195 us -> 0 us
  local copies, waits for them, and re-layouts: 80.6 us -> 6.17 us
  Pallas kernels: 0 us -> 72.6 us
  matrix products: 44.3 us -> 0 us
  other arithmetic: 41.7 us -> 0 us
  between operations: 14.6 us -> 1.3 us
    reduce_scatter x2 -> x0, waiting for transfers between devices: 116 us -> none  [the longest x1 64.2 us: local(): lax.psum_scatter(key_partial, 'grp', scatter_dimension=0, tiled=True)]
    all_gather x2 -> x0, waiting for transfers between devices: 78.5 us -> none  [the longest x1 42.5 us: local(): lax.all_gather(prompt_value_rows, 'grp', axis=0, tiled=True)]
    pallas_call x0 -> x1, Pallas kernels: none -> 72.6 us  [local(): pl.pallas_call(kernel, out_shape=(jax.ShapeDtypeStruct((WIDTH, 2048), f32...]
    dynamic_slice x48 -> x0, local copies, waits for them, and re-layouts: 45.3 us -> none  [the longest x16 15.8 us: one_block(): lax.dynamic_slice_in_dim(rows_of_keys, offset, prompt_block_rows, 0)]
    dot_general x117 -> x0, matrix products: 44.3 us -> none  [the longest x33 13.9 us: grad_dot_of(): jnp.einsum('rkgd,lkd->kgrl', gradient_split, head_values, preferred_eleme...]
    reduce_sum x49 -> x0, other arithmetic: 27.6 us -> none  [the longest x32 22.6 us: prompt_seen(): jnp.sum(jnp.where(slot_ids[:, None] == tile_ids[None, :], slot_seen[None,...]
    dynamic_update_slice x48 -> x0, local copies, waits for them, and re-layouts: 17.4 us -> none  [the longest x32 15.3 us: compute(): lax.dynamic_update_slice_in_dim(partial_value[2], value_part, offset, 0)]
    lt x17 -> x0, other arithmetic: 10.4 us -> none  [local(): live_rows = position < lengths[0]]
  transfers between devices with their start and end apart: 4 -> 0, of which waited for: 4 -> 0; matrix products, arithmetic and copies ran while one was open for 4% -> 0% of each run, Pallas kernels for 0% -> 0%
where the time goes in v1:
time: 80.3 us; the launch traced here: 80 us
  Pallas kernels  72.6 us (90%)
  local copies, waits for them, and re-layouts  6.17 us (8%)
  between operations  1.3 us (2%)
    pallas_call x1, Pallas kernels, local(): pl.pallas_call(kernel, out_shape=(jax.ShapeDtypeStruct((WIDTH, 2048), f32...  72.6 us
    unnamed x13, local copies, waits for them, and re-layouts  6.17 us

profile of v1, /device:TPU:1, one launch (start us, length us, event | category | flops | bytes accessed | tf_op | source)
XLA Modules:
  0.0 80.0 jit_solution(2208702001281507878)
XLA Ops:
  1.3 72.6 %tree_attention_backward.1 = (f32[128,2048]{1,0:T(8,128)}, f32[128,512]{1,0:T(8,128)}, f32[128,512]{1,0:T(8,128)}, f32[128,512]{1,0:T(8,128)}, f32[128,512]{1,0:T(8,128)}) custom-call(bf16[128,2048]{1,0:T(8,128)(2,1)} %q_ref.1, bf16[128,2048]{1,0:T(8,128)(2,1)} %og_ref.1, bf16[128,512]{1,0:T(8,128)(2,1)} %rk_ref.1, bf16[128,512]{1,0:T(8,128)(2,1)} %rv_ref.1, ...), custom_call_target="tpu_custom_call" | custom-call | tf_op jit(solution)/shard_map/tree_attention_backward/pallas_call | solution.py:402
  73.9 0.0 copy-start.3
  73.9 2.3 %copy.20 = f32[128,2048]{1,0:T(8,128)} copy(f32[128,2048]{1,0:T(8,128)} %get-tuple-element.10) | data formatting | bytes 2097152
  76.2 0.0 copy-done.3
  76.2 0.0 copy-start.2
  76.2 0.7 copy.21
  76.9 0.3 copy-done.2
  77.2 0.0 copy-start.1
  77.3 0.7 copy.22
  78.0 0.3 copy-done.1
  78.3 0.0 copy-start
  78.3 0.7 copy.23
  79.0 0.3 copy-done
  79.3 0.7 copy.24
Async XLA Ops:
  73.9 2.4 %copy-start.3 = (f32[128,512]{1,0:T(8,128)S(1)}, f32[128,512]{1,0:T(8,128)}, u32[]{:S(2)}) copy-start(f32[128,512]{1,0:T(8,128)} %get-tuple-element.11) | copy-start | bytes 786436
  76.2 1.0 %copy-start.2 = (f32[128,512]{1,0:T(8,128)S(1)}, f32[128,512]{1,0:T(8,128)}, u32[]{:S(2)}) copy-start(f32[128,512]{1,0:T(8,128)} %get-tuple-element.12) | copy-start | bytes 786436
  77.2 1.0 %copy-start.1 = (f32[128,512]{1,0:T(8,128)S(1)}, f32[128,512]{1,0:T(8,128)}, u32[]{:S(2)}) copy-start(f32[128,512]{1,0:T(8,128)} %get-tuple-element.13) | copy-start | bytes 786436
  78.3 1.0 %copy-start = (f32[128,512]{1,0:T(8,128)S(1)}, f32[128,512]{1,0:T(8,128)}, u32[]{:S(2)}) copy-start(f32[128,512]{1,0:T(8,128)} %get-tuple-element.14) | copy-start | bytes 786436

commit v2 on v1

v2 whole, which is shorter than its diff:
```python
import functools
import math

import jax
import jax.numpy as jnp
from jax import lax
from jax.experimental import pallas as pl
from jax.experimental.pallas import tpu as pltpu
from jax.sharding import PartitionSpec as P

MESH = pl.DeviceIdType.MESH
WIDTH = 128
RING = 8
HEADS = 2
MEMBERS = 4
HALF = MEMBERS * WIDTH
ROWS = 2 * HALF
CHUNK = 2 * WIDTH
LANES = 512
UP, DOWN = 0, 1
KEY, VALUE = 0, 1
HOPS = ((4, 3), (3, 4))
ROOT = 1.0 / math.sqrt(WIDTH)
SCALE = ROOT * math.log2(math.e)
HIDDEN = -1e30
MIB = 1024 * 1024


def dot_nt(a, b):
    return lax.dot_general(a, b, (((1,), (1,)), ((), ())), preferred_element_type=jnp.float32)


def dot_nn(a, b):
    return jnp.dot(a, b, preferred_element_type=jnp.float32)


def dot_tn(a, b):
    return lax.dot_general(a, b, (((0,), (0,)), ((), ())), preferred_element_type=jnp.float32)


def slot_of(direction, hop):
    return hop if direction == UP else RING - hop


def kernel(
    q_ref, og_ref, rk_ref, rv_ref, pk_ref, pv_ref, len_ref, mask_ref, order_ref,
    dq_out, drk_out, drv_out, dpk_out, dpv_out,
    qin, oin, rkin, rvin, meta, qs, os_, kv,
    e_buf, d_buf, er_buf, dr_buf, m_run, l_run, w_run, m_save, mr_save, p_tmp, ds_tmp,
    grad, sbuf, rbuf, fin, mate_grad, dq_t, dq_stage, drk_stage, drv_stage,
    loc_sem, send_sem, pair_recv, ag_recv, rs_recv,
):
    me = lax.axis_index("grp")
    z, c = me // 2, me % 2
    other = 1 - c
    above, below = (z + 1) % RING, (z + RING - 1) % RING
    straight = (above * 2 + c, below * 2 + c)
    cross = (above * 2 + other, below * 2 + other)
    mate = z * 2 + other
    mine = c
    theirs = 1 - mine

    def remote(src, dst, send, recv, target):
        return pltpu.make_async_remote_copy(
            src_ref=src, dst_ref=dst, send_sem=send, recv_sem=recv,
            device_id={"grp": target}, device_id_type=MESH,
        )

    def cols(core, width, start=0, size=None):
        size = width if size is None else size
        return pl.ds(pl.multiple_of(core * width + start, WIDTH), size)

    def half(core):
        return pl.ds(pl.multiple_of(core * WIDTH, WIDTH), WIDTH)

    prompt = (pk_ref, pv_ref)

    local = [
        pltpu.make_async_copy(q_ref.at[:, cols(mine, 1024)], qin.at[0], loc_sem),
        pltpu.make_async_copy(og_ref.at[:, cols(mine, 1024)], oin.at[0], loc_sem),
        pltpu.make_async_copy(rk_ref.at[:, cols(mine, 256)], rkin.at[0], loc_sem),
        pltpu.make_async_copy(rv_ref.at[:, cols(mine, 256)], rvin.at[0], loc_sem),
    ]
    for t in range(2):
        for hh in range(HEADS):
            local.append(
                pltpu.make_async_copy(
                    prompt[t].at[:, cols(mine, 256, hh * WIDTH, WIDTH)],
                    kv.at[t, hh, 0, half(c)],
                    loc_sem,
                )
            )
    for copy in local:
        copy.start()

    barrier = pltpu.get_barrier_semaphore()
    for target in (*straight, *cross, mate):
        pl.semaphore_signal(barrier, inc=1, device_id={"grp": target}, device_id_type=MESH)
    pl.semaphore_wait(barrier, 5)

    def start(copy):
        copy.start()

    streams = ((KEY, UP), (VALUE, DOWN), (VALUE, UP), (KEY, DOWN))

    def first_hop(hh, which=streams):
        for t, d in which:
            for heads, target in ((mine, straight[d]), (theirs, cross[d])):
                start(
                    remote(
                        prompt[t].at[:, cols(heads, 256, hh * WIDTH, WIDTH)],
                        kv.at[t, hh, slot_of(d, 1), half(c)],
                        send_sem.at[0],
                        ag_recv.at[t, hh, d, 0],
                        target,
                    )
                )

    def pair(i, src, dst, send=2):
        start(remote(src, dst, send_sem.at[send], pair_recv.at[i], mate))

    def arrival(ref, sem):
        pltpu.make_async_copy(ref, ref, sem).wait()

    first_hop(0)
    pair(0, rk_ref.at[:, cols(theirs, 256)], rkin.at[1])
    pair(0, rv_ref.at[:, cols(theirs, 256)], rvin.at[1])
    pair(0, q_ref.at[:, cols(theirs, 1024)], qin.at[1])
    pair(0, og_ref.at[:, cols(theirs, 1024)], oin.at[1])
    for t in range(2):
        for hh in range(HEADS):
            pair(1, prompt[t].at[:, cols(theirs, 256, hh * WIDTH, WIDTH)], kv.at[t, hh, 0, half(c)])
    first_hop(1, streams[:2])

    for s in range(16):
        seen = mask_ref[0, order_ref[s]]
        row = jnp.full((1, LANES), seen, jnp.int32).astype(jnp.float32)
        meta[0, pl.ds(s, 1), :] = (1.0 - jnp.minimum(row, 1.0)) * HIDDEN
    meta[0, pl.ds(16, 8), :] = jnp.full((8, LANES), len_ref[0], jnp.int32).astype(jnp.float32)
    pair(2, meta.at[0], meta.at[1], send=3)

    arrival(kv.at[:, :, :3], loc_sem)
    arrival(kv.at[:, 0, :5], pair_recv.at[0])
    arrival(meta.at[1], pair_recv.at[2])

    for hh in range(HEADS):
        for p in range(2):
            for g in range(MEMBERS):
                rows = pl.ds(p * HALF + g * WIDTH, WIDTH)
                lanes = pl.ds((hh * MEMBERS + g) * WIDTH, WIDTH)
                qs[hh, rows, :] = qin[p, :, lanes]
                os_[hh, rows, :] = oin[p, :, lanes]

    def own_block(hh):
        for p in range(2):
            keys = rkin[p, :, pl.ds(hh * WIDTH, WIDTH)]
            values = rvin[p, :, pl.ds(hh * WIDTH, WIDTH)]

            for b in range(HALF // LANES):
                lanes = pl.ds(b * LANES, LANES)
                rows = pl.ds(p * HALF + b * LANES, LANES)
                s = dot_nt(keys, qs[hh, rows, :])
                dp = dot_nt(values, os_[hh, rows, :])
                key_at = lax.broadcasted_iota(jnp.int32, (WIDTH, LANES), 0)
                row_at = lax.broadcasted_iota(jnp.int32, (WIDTH, LANES), 1) % WIDTH
                s = jnp.where(key_at <= row_at, s * SCALE, HIDDEN)
                top = jnp.max(s, axis=0, keepdims=True)
                e = jnp.exp2(s - top)
                er_buf[hh, p, :, lanes] = e
                dr_buf[hh, p, :, lanes] = dp
                m_run[hh, :, rows] = top
                mr_save[hh, :, rows] = top
                l_run[hh, :, rows] = jnp.sum(e, axis=0, keepdims=True)
                w_run[hh, :, rows] = jnp.sum(e * dp, axis=0, keepdims=True)

    def tile_bias(p, slot, part):
        tile = ((z + RING - slot) % RING) * 2 + part
        return meta[p, pl.ds(tile, 1), :]

    def forward(hh, slot):
        for p in range(2):
            bias = [tile_bias(p, slot, part) for part in range(2)]

            for b in range(HALF // LANES):
                lanes = pl.ds(p * HALF + b * LANES, LANES)
                s = dot_nt(kv[KEY, hh, slot], qs[hh, lanes, :])
                dp = dot_nt(kv[VALUE, hh, slot], os_[hh, lanes, :])
                d_buf[hh, slot, :, lanes] = dp
                old = m_run[hh, :, lanes]
                top = old
                for part in range(2):
                    high = jnp.max(s[part * WIDTH : (part + 1) * WIDTH], axis=0, keepdims=True)
                    top = jnp.maximum(top, high * SCALE + bias[part])
                less = jnp.exp2(old - top)
                total = l_run[hh, :, lanes] * less
                weighted = w_run[hh, :, lanes] * less
                for part in range(2):
                    rows = slice(part * WIDTH, (part + 1) * WIDTH)
                    e = jnp.exp2(s[rows] * SCALE - (top - bias[part]))
                    e_buf[hh, slot, rows, lanes] = e
                    total = total + jnp.sum(e, axis=0, keepdims=True)
                    weighted = weighted + jnp.sum(e * dp[rows], axis=0, keepdims=True)
                m_run[hh, :, lanes] = top
                m_save[hh, slot, :, lanes] = top
                l_run[hh, :, lanes] = total
                w_run[hh, :, lanes] = weighted

    def gather(hh, hop, which=streams):
        for t, d in which:
            if hop > HOPS[t][d]:
                continue
            here = kv.at[t, hh, slot_of(d, hop)]
            arrival(here, ag_recv.at[t, hh, d, hop - 1])
            if hop < HOPS[t][d]:
                start(
                    remote(
                        here,
                        kv.at[t, hh, slot_of(d, hop + 1)],
                        send_sem.at[0],
                        ag_recv.at[t, hh, d, hop],
                        straight[d],
                    )
                )

    def settle(hh):
        for p in range(2):
            for b in range(HALF // LANES):
                lanes = pl.ds(p * HALF + b * LANES, LANES)
                total = l_run[hh, :, lanes]
                w_run[hh, :, lanes] = w_run[hh, :, lanes] / total
                at = (lax.broadcasted_iota(jnp.int32, (1, LANES), 1) % WIDTH).astype(jnp.float32)
                live = at < meta[p, pl.ds(16, 1), :]
                l_run[hh, :, lanes] = jnp.where(live, 1.0 / total, 0.0)

    def backward(hh, slot):
        keys = kv[KEY, hh, slot].T

        for b in range(ROWS // LANES):
            lanes = pl.ds(b * LANES, LANES)
            factor = jnp.exp2(m_save[hh, slot, :, lanes] - m_run[hh, :, lanes]) * l_run[hh, :, lanes]
            prob = e_buf[hh, slot, :, lanes] * factor
            p_tmp[:, lanes] = prob.astype(jnp.bfloat16)
            ds = (prob * (d_buf[hh, slot, :, lanes] - w_run[hh, :, lanes])).astype(jnp.bfloat16)
            ds_tmp[:, lanes] = ds
            turned = dot_nn(keys, ds)
            dq_t[hh, :, lanes] = turned if slot == 4 else dq_t[hh, :, lanes] + turned

        grad[KEY, hh, slot] = dot_nn(ds_tmp[...], qs[hh])
        grad[VALUE, hh, slot] = dot_nn(p_tmp[...], os_[hh])

    def pass_on(t, hh, d, hop, slot):
        i = hop - 1
        if hop == 1:
            sbuf[t, hh, d, i] = grad[t, hh, slot].astype(jnp.bfloat16)
        else:
            arrived = rbuf.at[t, hh, d, i - 1]
            arrival(arrived, rs_recv.at[t, hh, d, i - 1])
            sbuf[t, hh, d, i] = (grad[t, hh, slot] + arrived[...].astype(jnp.float32)).astype(jnp.bfloat16)
        if hop < HOPS[t][d]:
            start(
                remote(
                    sbuf.at[t, hh, d, i],
                    rbuf.at[t, hh, d, i],
                    send_sem.at[1],
                    rs_recv.at[t, hh, d, i],
                    straight[d],
                )
            )
        else:
            for way, (core, target) in enumerate(((c, straight[d]), (other, cross[d]))):
                start(
                    remote(
                        sbuf.at[t, hh, d, i, half(core)],
                        fin.at[t, hh, d, way],
                        send_sem.at[1],
                        rs_recv.at[t, hh, d, 3],
                        target,
                    )
                )

    def scatter(hh, away, first=None):
        for t, d in streams:
            hop = HOPS[t][d] - away + 1
            if hop > 0 and first in (None, hop == 1):
                pass_on(t, hh, d, hop, RING - away if d == UP else away)

    def own_chunk(hh):
        backward(hh, 0)
        for t in range(2):
            pair(3 + hh, grad.at[t, hh, 0, half(other)], mate_grad.at[hh, t])

    def own_tokens(hh):
        lanes = pl.ds(hh * WIDTH, WIDTH)
        for p in range(2):
            rows = pl.ds(p * HALF, HALF)
            factor = jnp.exp2(mr_save[hh, :, rows] - m_run[hh, :, rows]) * l_run[hh, :, rows]
            prob = er_buf[hh, p] * factor
            ds = (prob * (dr_buf[hh, p] - w_run[hh, :, rows])).astype(jnp.bfloat16)
            dq_t[hh, :, rows] += dot_tn(rkin[p, :, lanes], ds)
            key_part = dot_nn(ds, qs[hh, rows, :]) * ROOT
            value_part = dot_nn(prob.astype(jnp.bfloat16), os_[hh, rows, :])
            if p == 0:
                drk_out[:, cols(mine, 256, hh * WIDTH, WIDTH)] = key_part
                drv_out[:, cols(mine, 256, hh * WIDTH, WIDTH)] = value_part
            else:
                drk_stage[:, lanes] = key_part
                drv_stage[:, lanes] = value_part

    def give_own():
        for stage, out in ((drk_stage, drk_out), (drv_stage, drv_out)):
            pair(5, stage, out.at[:, cols(mine, 256)])

    def give_query(hh):
        for p in (1, 0):
            for g in range(MEMBERS):
                block = dq_t[hh, :, pl.ds(p * HALF + g * WIDTH, WIDTH)].T * ROOT
                if p == 0:
                    dq_out[:, cols(mine, 1024, (hh * MEMBERS + g) * WIDTH, WIDTH)] = block
                else:
                    dq_stage[:, pl.ds((hh * MEMBERS + g) * WIDTH, WIDTH)] = block
            if p == 1:
                pair(
                    5,
                    dq_stage.at[:, pl.ds(hh * HALF, HALF)],
                    dq_out.at[:, cols(mine, 1024, hh * HALF, HALF)],
                )

    result = (dpk_out, dpv_out)

    def finish(hh):
        arrival(mate_grad.at[hh], pair_recv.at[3 + hh])
        for t in range(2):
            for d in (UP, DOWN):
                arrival(fin.at[t, hh, d], rs_recv.at[t, hh, d, 3])
            for way, heads in enumerate((mine, theirs)):
                share = grad[t, hh, 0, half(c), :] if way == 0 else mate_grad[hh, t]
                for d in (UP, DOWN):
                    share = share + fin[t, hh, d, way].astype(jnp.float32)
                if t == KEY:
                    share = share * ROOT
                result[t][:, cols(heads, 256, hh * WIDTH, WIDTH)] = share

    own_block(0)
    own_block(1)
    arrival(kv.at[0, 0, :2], pair_recv.at[1])
    forward(0, 0)
    gather(0, 1)
    first_hop(1, streams[2:])
    forward(1, 0)
    forward(0, 1)
    forward(0, 7)
    gather(1, 1, streams[:2])
    gather(0, 2)
    gather(1, 1, streams[2:])
    forward(0, 2)
    forward(0, 6)
    forward(1, 1)
    forward(1, 7)
    gather(1, 2, streams[:2])
    gather(0, 3)
    gather(1, 2, streams[2:])
    forward(0, 3)
    forward(0, 5)
    forward(1, 2)
    forward(1, 6)
    gather(1, 3, streams[:2])
    gather(0, 4)
    forward(0, 4)
    settle(0)
    backward(0, 4)
    scatter(0, 4)
    gather(1, 3, streams[2:])
    backward(0, 5)
    backward(0, 3)
    scatter(0, 3, True)
    forward(1, 3)
    forward(1, 5)
    gather(1, 4)
    forward(1, 4)
    settle(1)
    backward(1, 4)
    scatter(1, 4)
    scatter(0, 3, False)
    backward(1, 5)
    backward(1, 3)
    scatter(1, 3, True)
    backward(0, 6)
    backward(0, 2)
    scatter(1, 3, False)
    scatter(0, 2)
    backward(1, 6)
    backward(1, 2)
    backward(0, 7)
    backward(0, 1)
    scatter(1, 2)
    scatter(0, 1)
    own_tokens(0)
    own_tokens(1)
    give_own()
    backward(1, 7)
    backward(1, 1)
    scatter(1, 1)
    own_chunk(0)
    own_chunk(1)
    give_query(0)
    give_query(1)
    finish(0)
    finish(1)

    arrival(kv.at[:, :, :3], pair_recv.at[5])
    for i in range(3):
        arrival(kv.at[:, :, :7], send_sem.at[i])
    arrival(meta.at[1], send_sem.at[3])


def deliver(*refs):
    given, out, sem = refs[:5], refs[5:10], refs[10]
    copies = [pltpu.make_async_copy(given[i], out[i], sem.at[i]) for i in range(5)]
    for copy in copies:
        copy.start()
    for copy in copies:
        copy.wait()


def local(*args):
    bf16, f32 = jnp.bfloat16, jnp.float32
    vmem = pltpu.VMEM
    dma = pltpu.SemaphoreType.DMA
    any_ = pl.BlockSpec(memory_space=pl.ANY)
    smem = pl.BlockSpec(memory_space=pltpu.SMEM)
    in_vmem = pl.BlockSpec(memory_space=pltpu.VMEM)
    shapes = [(WIDTH, 2048)] + [(WIDTH, 512)] * 4
    inside = pl.pallas_call(
        kernel,
        out_shape=[pltpu.VMEM(shape, f32) for shape in shapes],
        in_specs=[any_] * 6 + [smem] * 3,
        out_specs=[in_vmem] * 5,
        scratch_shapes=[
            vmem((2, WIDTH, 1024), bf16),
            vmem((2, WIDTH, 1024), bf16),
            vmem((2, WIDTH, 256), bf16),
            vmem((2, WIDTH, 256), bf16),
            vmem((2, 24, LANES), f32),
            vmem((HEADS, ROWS, WIDTH), bf16),
            vmem((HEADS, ROWS, WIDTH), bf16),
            vmem((2, HEADS, RING, CHUNK, WIDTH), bf16),
            vmem((HEADS, RING, CHUNK, ROWS), f32),
            vmem((HEADS, RING, CHUNK, ROWS), f32),
            vmem((HEADS, 2, WIDTH, HALF), f32),
            vmem((HEADS, 2, WIDTH, HALF), f32),
            vmem((HEADS, 1, ROWS), f32),
            vmem((HEADS, 1, ROWS), f32),
            vmem((HEADS, 1, ROWS), f32),
            vmem((HEADS, RING, 1, ROWS), f32),
            vmem((HEADS, 1, ROWS), f32),
            vmem((CHUNK, ROWS), bf16),
            vmem((CHUNK, ROWS), bf16),
            vmem((2, HEADS, RING, CHUNK, WIDTH), f32),
            vmem((2, HEADS, 2, 4, CHUNK, WIDTH), bf16),
            vmem((2, HEADS, 2, 3, CHUNK, WIDTH), bf16),
            vmem((2, HEADS, 2, 2, WIDTH, WIDTH), bf16),
            vmem((HEADS, 2, WIDTH, WIDTH), f32),
            vmem((HEADS, WIDTH, ROWS), f32),
            vmem((WIDTH, 1024), f32),
            vmem((WIDTH, 256), f32),
            vmem((WIDTH, 256), f32),
            pltpu.SemaphoreType.DMA,
            dma((4,)),
            dma((6,)),
            dma((2, HEADS, 2, 4)),
            dma((2, HEADS, 2, 4)),
        ],
        compiler_params=pltpu.CompilerParams(
            collective_id=0, has_side_effects=True, vmem_limit_bytes=54 * MIB
        ),
        name="tree_attention_backward",
    )(*args)
    return pl.pallas_call(
        deliver,
        out_shape=[jax.ShapeDtypeStruct(shape, f32) for shape in shapes],
        in_specs=[in_vmem] * 5,
        out_specs=[any_] * 5,
        scratch_shapes=[dma((5,))],
        compiler_params=pltpu.CompilerParams(vmem_limit_bytes=MIB),
        name="deliver",
    )(*inside)


def solution(mesh):
    rows = P(("dp", "grp"), "head")
    return jax.shard_map(
        local,
        mesh=mesh,
        in_specs=(rows,) * 6 + (P(("dp", "grp")), P(("dp", "grp"), None), P("dp")),
        out_specs=(rows,) * 5,
        check_vma=False,
    )
```

time: 80.3 us -> 54.7 us (0.68)
  Pallas kernels: 72.6 us -> 53.1 us
  local copies, waits for them, and re-layouts: 6.17 us -> 0 us
    pallas_call x1 -> x2, Pallas kernels: 72.6 us -> 53.1 us  [the longest x1 51.8 us: local(): pl.pallas_call(kernel, out_shape=[pltpu.VMEM(shape, f32) for shape in sha...]
    unnamed x13 -> x0, local copies, waits for them, and re-layouts: 6.17 us -> none
where the time goes in v2:
time: 54.7 us; the launch traced here: 54.6 us
  Pallas kernels  53.1 us (97%)
  between operations  1.45 us (3%)
    pallas_call x1, Pallas kernels, local(): pl.pallas_call(kernel, out_shape=[pltpu.VMEM(shape, f32) for shape in sha...  51.8 us
    pallas_call x1, Pallas kernels, local(): pl.pallas_call(deliver, out_shape=[jax.ShapeDtypeStruct(shape, f32) for s...  1.35 us

profile of v2, /device:TPU:1, one launch (start us, length us, event | category | flops | bytes accessed | tf_op | source)
XLA Modules:
  0.0 54.6 jit_solution(6144460491714093834)
XLA Ops:
  1.3 51.8 %tree_attention_backward.1 = (f32[128,2048]{1,0:T(8,128)S(1)}, f32[128,512]{1,0:T(8,128)S(1)}, f32[128,512]{1,0:T(8,128)S(1)}, f32[128,512]{1,0:T(8,128)S(1)}, f32[128,512]{1,0:T(8,128)S(1)}) custom-call(bf16[128,2048]{1,0:T(8,128)(2,1)} %q_ref.1, bf16[128,2048]{1,0:T(8,128)(2,1)} %og_ref.1, bf16[128,512]{1,0:T(8,128)(2,1)} %rk_ref.1, ...), custom_call_target="tpu_custom_call" | custom-call | tf_op jit(solution)/shard_map/tree_attention_backward/pallas_call | solution.py:433
  53.1 1.4 %deliver.1 = (f32[128,2048]{1,0:T(8,128)}, f32[128,512]{1,0:T(8,128)}, f32[128,512]{1,0:T(8,128)}, f32[128,512]{1,0:T(8,128)}, f32[128,512]{1,0:T(8,128)}) custom-call(f32[128,2048]{1,0:T(8,128)S(1)} %get-tuple-element.10.refs_0_, f32[128,512]{1,0:T(8,128)S(1)} %get-tuple-element.11.refs_1_, f32[128,512]{1,0:T(8,128)S(1)} %get-tuple-element.12.refs_2_, ...), custom_call_target="tpu_custom_call" | custom-call | tf_op jit(solution)/shard_map/deliver/pallas_call | solution.py:478

commit v3 on v2

--- a/solution.py
+++ b/solution.py
@@ -43,12 +43,12 @@
 
 
 def kernel(
-    q_ref, og_ref, rk_ref, rv_ref, pk_ref, pv_ref, len_ref, mask_ref, order_ref,
+    q_ref, og_ref, rk_ref, rv_ref, pk_ref, pv_ref, len_in, mask_in, order_in,
     dq_out, drk_out, drv_out, dpk_out, dpv_out,
     qin, oin, rkin, rvin, meta, qs, os_, kv,
-    e_buf, d_buf, er_buf, dr_buf, m_run, l_run, w_run, m_save, mr_save, p_tmp, ds_tmp,
+    e_buf, d_buf, er_buf, dr_buf, m_run, l_run, w_run, m_save, mr_save,
     grad, sbuf, rbuf, fin, mate_grad, dq_t, dq_stage, drk_stage, drv_stage,
-    loc_sem, send_sem, pair_recv, ag_recv, rs_recv,
+    len_ref, mask_ref, order_ref, loc_sem, small_sem, send_sem, pair_recv, ag_recv, rs_recv,
 ):
     me = lax.axis_index("grp")
     z, c = me // 2, me % 2
@@ -72,6 +72,10 @@
 
     def half(core):
         return pl.ds(pl.multiple_of(core * WIDTH, WIDTH), WIDTH)
+
+    barrier = pltpu.get_barrier_semaphore()
+    for target in (*straight, *cross, mate):
+        pl.semaphore_signal(barrier, inc=1, device_id={"grp": target}, device_id_type=MESH)
 
     prompt = (pk_ref, pv_ref)
 
@@ -90,12 +94,13 @@
                     loc_sem,
                 )
             )
-    for copy in local:
+    small = [
+        pltpu.make_async_copy(src, dst, small_sem.at[i])
+        for i, (src, dst) in enumerate(((len_in, len_ref), (mask_in, mask_ref), (order_in, order_ref)))
+    ]
+    for copy in local + small:
         copy.start()
 
-    barrier = pltpu.get_barrier_semaphore()
-    for target in (*straight, *cross, mate):
-        pl.semaphore_signal(barrier, inc=1, device_id={"grp": target}, device_id_type=MESH)
     pl.semaphore_wait(barrier, 5)
 
     def start(copy):
@@ -132,6 +137,8 @@
             pair(1, prompt[t].at[:, cols(theirs, 256, hh * WIDTH, WIDTH)], kv.at[t, hh, 0, half(c)])
     first_hop(1, streams[:2])
 
+    for copy in small:
+        copy.wait()
     for s in range(16):
         seen = mask_ref[0, order_ref[s]]
         row = jnp.full((1, LANES), seen, jnp.int32).astype(jnp.float32)
@@ -177,33 +184,37 @@
         tile = ((z + RING - slot) % RING) * 2 + part
         return meta[p, pl.ds(tile, 1), :]
 
-    def forward(hh, slot):
+    def rows_of(kind, hh, slots):
+        return jnp.concatenate([kv[kind, hh, slot] for slot in slots], axis=0)
+
+    def forward(hh, *slots):
+        tiles = [(n, slot, part) for n, slot in enumerate(slots) for part in range(2)]
         for p in range(2):
-            bias = [tile_bias(p, slot, part) for part in range(2)]
-
-            for b in range(HALF // LANES):
-                lanes = pl.ds(p * HALF + b * LANES, LANES)
-                s = dot_nt(kv[KEY, hh, slot], qs[hh, lanes, :])
-                dp = dot_nt(kv[VALUE, hh, slot], os_[hh, lanes, :])
-                d_buf[hh, slot, :, lanes] = dp
-                old = m_run[hh, :, lanes]
-                top = old
-                for part in range(2):
-                    high = jnp.max(s[part * WIDTH : (part + 1) * WIDTH], axis=0, keepdims=True)
-                    top = jnp.maximum(top, high * SCALE + bias[part])
-                less = jnp.exp2(old - top)
-                total = l_run[hh, :, lanes] * less
-                weighted = w_run[hh, :, lanes] * less
-                for part in range(2):
-                    rows = slice(part * WIDTH, (part + 1) * WIDTH)
-                    e = jnp.exp2(s[rows] * SCALE - (top - bias[part]))
-                    e_buf[hh, slot, rows, lanes] = e
-                    total = total + jnp.sum(e, axis=0, keepdims=True)
-                    weighted = weighted + jnp.sum(e * dp[rows], axis=0, keepdims=True)
-                m_run[hh, :, lanes] = top
+            lanes = pl.ds(p * HALF, HALF)
+            s = dot_nt(rows_of(KEY, hh, slots), qs[hh, lanes, :])
+            dp = dot_nt(rows_of(VALUE, hh, slots), os_[hh, lanes, :])
+            for n, slot in enumerate(slots):
+                d_buf[hh, slot, :, lanes] = dp[n * CHUNK : (n + 1) * CHUNK]
+            old = m_run[hh, :, lanes]
+            top = old
+            for n, slot, part in tiles:
+                rows = slice(n * CHUNK + part * WIDTH, n * CHUNK + (part + 1) * WIDTH)
+                high = jnp.max(s[rows], axis=0, keepdims=True)
+                top = jnp.maximum(top, high * SCALE + tile_bias(p, slot, part))
+            less = jnp.exp2(old - top)
+            total = l_run[hh, :, lanes] * less
+            weighted = w_run[hh, :, lanes] * less
+            for n, slot, part in tiles:
+                rows = slice(n * CHUNK + part * WIDTH, n * CHUNK + (part + 1) * WIDTH)
+                e = jnp.exp2(s[rows] * SCALE - (top - tile_bias(p, slot, part)))
+                e_buf[hh, slot, pl.ds(part * WIDTH, WIDTH), lanes] = e
+                total = total + jnp.sum(e, axis=0, keepdims=True)
+                weighted = weighted + jnp.sum(e * dp[rows], axis=0, keepdims=True)
+            m_run[hh, :, lanes] = top
+            for slot in slots:
                 m_save[hh, slot, :, lanes] = top
-                l_run[hh, :, lanes] = total
-                w_run[hh, :, lanes] = weighted
+            l_run[hh, :, lanes] = total
+            w_run[hh, :, lanes] = weighted
 
     def gather(hh, hop, which=streams):
         for t, d in which:
@@ -232,21 +243,25 @@
                 live = at < meta[p, pl.ds(16, 1), :]
                 l_run[hh, :, lanes] = jnp.where(live, 1.0 / total, 0.0)
 
-    def backward(hh, slot):
-        keys = kv[KEY, hh, slot].T
-
-        for b in range(ROWS // LANES):
-            lanes = pl.ds(b * LANES, LANES)
-            factor = jnp.exp2(m_save[hh, slot, :, lanes] - m_run[hh, :, lanes]) * l_run[hh, :, lanes]
-            prob = e_buf[hh, slot, :, lanes] * factor
-            p_tmp[:, lanes] = prob.astype(jnp.bfloat16)
-            ds = (prob * (d_buf[hh, slot, :, lanes] - w_run[hh, :, lanes])).astype(jnp.bfloat16)
-            ds_tmp[:, lanes] = ds
+    def backward(hh, *slots):
+        keys = rows_of(KEY, hh, slots).T
+        for p in range(2):
+            lanes = pl.ds(p * HALF, HALF)
+            probs, scores = [], []
+            for slot in slots:
+                factor = jnp.exp2(m_save[hh, slot, :, lanes] - m_run[hh, :, lanes]) * l_run[hh, :, lanes]
+                prob = e_buf[hh, slot, :, lanes] * factor
+                probs.append(prob.astype(jnp.bfloat16))
+                ds = prob * (d_buf[hh, slot, :, lanes] - w_run[hh, :, lanes])
+                scores.append(ds.astype(jnp.bfloat16))
+            ds = jnp.concatenate(scores, axis=0)
+            parts = (dot_nn(ds, qs[hh, lanes, :]), dot_nn(jnp.concatenate(probs, axis=0), os_[hh, lanes, :]))
+            for t in (KEY, VALUE):
+                for n, slot in enumerate(slots):
+                    part = parts[t][n * CHUNK : (n + 1) * CHUNK]
+                    grad[t, hh, slot] = part if p == 0 else grad[t, hh, slot] + part
             turned = dot_nn(keys, ds)
-            dq_t[hh, :, lanes] = turned if slot == 4 else dq_t[hh, :, lanes] + turned
-
-        grad[KEY, hh, slot] = dot_nn(ds_tmp[...], qs[hh])
-        grad[VALUE, hh, slot] = dot_nn(p_tmp[...], os_[hh])
+            dq_t[hh, :, lanes] = turned if slots[0] == 4 else dq_t[hh, :, lanes] + turned
 
     def pass_on(t, hh, d, hop, slot):
         i = hop - 1
@@ -347,22 +362,17 @@
     gather(0, 1)
     first_hop(1, streams[2:])
     forward(1, 0)
-    forward(0, 1)
-    forward(0, 7)
+    forward(0, 1, 7)
     gather(1, 1, streams[:2])
     gather(0, 2)
     gather(1, 1, streams[2:])
-    forward(0, 2)
-    forward(0, 6)
-    forward(1, 1)
-    forward(1, 7)
+    forward(0, 2, 6)
+    forward(1, 1, 7)
     gather(1, 2, streams[:2])
     gather(0, 3)
     gather(1, 2, streams[2:])
-    forward(0, 3)
-    forward(0, 5)
-    forward(1, 2)
-    forward(1, 6)
+    forward(0, 3, 5)
+    forward(1, 2, 6)
     gather(1, 3, streams[:2])
     gather(0, 4)
     forward(0, 4)
@@ -370,35 +380,28 @@
     backward(0, 4)
     scatter(0, 4)
     gather(1, 3, streams[2:])
-    backward(0, 5)
-    backward(0, 3)
+    backward(0, 5, 3)
     scatter(0, 3, True)
-    forward(1, 3)
-    forward(1, 5)
+    forward(1, 3, 5)
     gather(1, 4)
     forward(1, 4)
     settle(1)
     backward(1, 4)
     scatter(1, 4)
     scatter(0, 3, False)
-    backward(1, 5)
-    backward(1, 3)
+    backward(1, 5, 3)
     scatter(1, 3, True)
-    backward(0, 6)
-    backward(0, 2)
+    backward(0, 6, 2)
     scatter(1, 3, False)
     scatter(0, 2)
-    backward(1, 6)
-    backward(1, 2)
-    backward(0, 7)
-    backward(0, 1)
+    backward(1, 6, 2)
+    backward(0, 7, 1)
     scatter(1, 2)
     scatter(0, 1)
     own_tokens(0)
     own_tokens(1)
     give_own()
-    backward(1, 7)
-    backward(1, 1)
+    backward(1, 7, 1)
     scatter(1, 1)
     own_chunk(0)
     own_chunk(1)
@@ -427,13 +430,12 @@
     vmem = pltpu.VMEM
     dma = pltpu.SemaphoreType.DMA
     any_ = pl.BlockSpec(memory_space=pl.ANY)
-    smem = pl.BlockSpec(memory_space=pltpu.SMEM)
     in_vmem = pl.BlockSpec(memory_space=pltpu.VMEM)
     shapes = [(WIDTH, 2048)] + [(WIDTH, 512)] * 4
     inside = pl.pallas_call(
         kernel,
         out_shape=[pltpu.VMEM(shape, f32) for shape in shapes],
-        in_specs=[any_] * 6 + [smem] * 3,
+        in_specs=[any_] * 9,
         out_specs=[in_vmem] * 5,
         scratch_shapes=[
             vmem((2, WIDTH, 1024), bf16),
@@ -453,8 +455,6 @@
             vmem((HEADS, 1, ROWS), f32),
             vmem((HEADS, RING, 1, ROWS), f32),
             vmem((HEADS, 1, ROWS), f32),
-            vmem((CHUNK, ROWS), bf16),
-            vmem((CHUNK, ROWS), bf16),
             vmem((2, HEADS, RING, CHUNK, WIDTH), f32),
             vmem((2, HEADS, 2, 4, CHUNK, WIDTH), bf16),
             vmem((2, HEADS, 2, 3, CHUNK, WIDTH), bf16),
@@ -464,7 +464,11 @@
             vmem((WIDTH, 1024), f32),
             vmem((WIDTH, 256), f32),
             vmem((WIDTH, 256), f32),
+            pltpu.SMEM((1,), jnp.int32),
+            pltpu.SMEM((1, 16), jnp.int32),
+            pltpu.SMEM((16,), jnp.int32),
             pltpu.SemaphoreType.DMA,
+            dma((3,)),
             dma((4,)),
             dma((6,)),
             dma((2, HEADS, 2, 4)),

time: 54.7 us -> 53.6 us (0.980)
  Pallas kernels: 53.1 us -> 52.1 us
    pallas_call x1, Pallas kernels: 51.8 us -> 50.7 us  [local(): pl.pallas_call(kernel, out_shape=[pltpu.VMEM(shape, f32) for shape in sha...]
where the time goes in v3:
time: 53.6 us; the launch traced here: 53.5 us
  Pallas kernels  52.1 us (97%)
  between operations  1.45 us (3%)
    pallas_call x1, Pallas kernels, local(): pl.pallas_call(kernel, out_shape=[pltpu.VMEM(shape, f32) for shape in sha...  50.7 us
    pallas_call x1, Pallas kernels, local(): pl.pallas_call(deliver, out_shape=[jax.ShapeDtypeStruct(shape, f32) for s...  1.35 us

profile of v3, /device:TPU:1, one launch (start us, length us, event | category | flops | bytes accessed | tf_op | source)
XLA Modules:
  0.0 53.5 jit_solution(13630299633480960980)
XLA Ops:
  1.3 50.7 %tree_attention_backward.1 = (f32[128,2048]{1,0:T(8,128)S(1)}, f32[128,512]{1,0:T(8,128)S(1)}, f32[128,512]{1,0:T(8,128)S(1)}, f32[128,512]{1,0:T(8,128)S(1)}, f32[128,512]{1,0:T(8,128)S(1)}) custom-call(bf16[128,2048]{1,0:T(8,128)(2,1)} %q_ref.1, bf16[128,2048]{1,0:T(8,128)(2,1)} %og_ref.1, bf16[128,512]{1,0:T(8,128)(2,1)} %rk_ref.1, ...), custom_call_target="tpu_custom_call" | custom-call | tf_op jit(solution)/shard_map/tree_attention_backward/pallas_call | solution.py:435
  52.0 1.4 %deliver.1 = (f32[128,2048]{1,0:T(8,128)}, f32[128,512]{1,0:T(8,128)}, f32[128,512]{1,0:T(8,128)}, f32[128,512]{1,0:T(8,128)}, f32[128,512]{1,0:T(8,128)}) custom-call(f32[128,2048]{1,0:T(8,128)S(1)} %get-tuple-element.10.refs_0_, f32[128,512]{1,0:T(8,128)S(1)} %get-tuple-element.11.refs_1_, f32[128,512]{1,0:T(8,128)S(1)} %get-tuple-element.12.refs_2_, ...), custom_call_target="tpu_custom_call" | custom-call | tf_op jit(solution)/shard_map/deliver/pallas_call | solution.py:482
